TPU v7x, 32 devices: a whole 2x2x4 slice. The times are simulated.
32 devices in a mesh: rows: 8 (over z, x), cols: 4 (over y, core).
Axes of the slice: x: 2, y: 2, z: 4, core: 2. Of those that a mesh axis runs over, the one named last changes fastest.
Arguments:
- matrix: float32 [16384, 1024], P('rows', 'cols'), may hold values from -80 to 80
- gaussian: float32 [256, 16384], P(None, 'rows'), may hold values from -0.0625 to 0.0625
- pivots: int32 [256], replicated, may hold values from 0 to 1023, as said below
- trailing: float32 [16384, 512], P('rows', 'cols'), may hold values from -6 to 6
Outputs:
- sketch: float32 [256, 1024], P('rows', 'cols')
- coupling: float32 [256, 512], P(None, 'cols')
- projected: float32 [16384, 512], P('rows', 'cols')
- trailing_sketch: float32 [256, 512], P('rows', 'cols')
Inputs may be any that keep to these rules, and one draw needn't show every extreme that they name: `pivots`: 256 distinct column indices; at most 64 of them lie in one block of 256 consecutive columns starting at a multiple of 256, and exactly 64 in some such block.
All inputs are finite; a program needn't handle non-finite values.
Results may differ from a plain program's by a relative error of at most 0.00015.
Values sent between devices are 32-bit elements; how exact they have to be, the bound alone decides.
A program may use at most 64 MiB of HBM per device.

v0:
```python
import jax
import jax.numpy as jnp
from jax import lax
from jax.sharding import PartitionSpec as P


def inner_rows(left, right):
    return lax.dot_general(
        left,
        right,
        (((0,), (0,)), ((), ())),
        precision=lax.Precision.HIGHEST,
        preferred_element_type=jnp.float32,
    )


def product(left, right):
    return jnp.dot(left, right, precision=lax.Precision.HIGHEST, preferred_element_type=jnp.float32)


def factor_parts(gram_matrix, cross_terms):
    chol_factor = jnp.linalg.cholesky(gram_matrix)
    coupling = lax.linalg.triangular_solve(chol_factor, cross_terms, left_side=True, lower=True)
    weights = lax.linalg.triangular_solve(
        chol_factor, coupling, left_side=True, lower=True, transpose_a=True
    )
    return (coupling, weights)


def shards(matrix, gaussian, pivots, trailing):
    rows_dev, cols_dev = matrix.shape
    sketch_rows = gaussian.shape[0]
    panel_width = pivots.shape[0]
    row_groups = lax.axis_size("rows")
    sketch_share = sketch_rows // row_groups
    row_start = lax.axis_index("rows") * sketch_share
    col_block = lax.axis_index("cols")
    sketch = lax.psum_scatter(product(gaussian, matrix), "rows", scatter_dimension=0, tiled=True)
    local_index = pivots - col_block * cols_dev
    selector = (
        lax.broadcasted_iota(jnp.int32, (cols_dev, panel_width), 0) == local_index[None, :]
    ).astype(jnp.float32)
    panel_block = lax.psum(product(matrix, selector), "cols")
    gram_matrix, cross_terms, gauss_panel, gauss_trail = lax.psum(
        (
            inner_rows(panel_block, panel_block),
            inner_rows(panel_block, trailing),
            product(gaussian, panel_block),
            product(gaussian, trailing),
        ),
        "rows",
    )
    coupling, weights = factor_parts(gram_matrix, cross_terms)
    projected = trailing - product(panel_block, weights)
    sketch_full = gauss_trail - product(gauss_panel, weights)
    trailing_sketch = lax.dynamic_slice_in_dim(sketch_full, row_start, sketch_share, 0)
    return (sketch, coupling, projected, trailing_sketch)


def solution(mesh):
    placed = (P("rows", "cols"), P(None, "rows"), P(), P("rows", "cols"))
    return jax.shard_map(
        shards,
        mesh=mesh,
        in_specs=placed,
        out_specs=(P("rows", "cols"), P(None, "cols"), P("rows", "cols"), P("rows", "cols")),
        check_vma=False,
    )
```

profile of v0, /device:TPU:0, one launch (start us, length us, event | category | flops | bytes accessed | tf_op | source)
XLA Modules:
  0.0 236.2 jit_solution(3058393348180474377)
XLA Ops:
  7.2 0.8 broadcast_subtract_fusion
  8.1 0.7 copy-done
  8.8 2.6 %convolution_bitcast_fusion = f32[2048,256]{0,1:T(8,128)} fusion(f32[2048,256]{1,0:T(8,128)S(1)} %copy-done, s32[256]{0:T(256)S(1)} %broadcast_subtract_fusion), kind=kOutput, calls=%fused_computation.2 | convolution fusion | flops 1610743808 | bytes 4195328 | tf_op jit(solution)/shard_map/dot_general | solution.py:18
  11.4 1.1 copy-done.3
  12.6 4.0 %fusion.21 = f32[256,128]{1,0:T(8,128)} fusion(f32[256,2048]{1,0:T(8,128)} %param.5, f32[2048,128]{1,0:T(8,128)S(1)} %copy-done.3), kind=kOutput, calls=%fused_computation.48 | convolution fusion | flops 805306368 | bytes 3276800 | tf_op jit(solution)/shard_map/dot_general | solution.py:18
  16.6 49.0 %all-reduce.5.cloned.1.call-done = f32[2048,256]{0,1:T(8,128)} async-done(((f32[2048,256]{0,1:T(8,128)}), f32[2048,256]{0,1:T(8,128)}) %all-reduce.5.cloned.1.call-update) | async-done | bytes 2097168 | tf_op jit(solution)/shard_map/psum | solution.py:43
  65.6 5.0 %convolution_bitcast_fusion.1 = f32[256,256]{0,1:T(8,128)} fusion(f32[2048,256]{0,1:T(8,128)} %all-reduce.5.cloned.1.call-done, f32[256,2048]{1,0:T(8,128)} %param.5), kind=kOutput, calls=%fused_computation.4 | convolution fusion | flops 1610612736 | bytes 4456448 | tf_op jit(solution)/shard_map/dot_general | solution.py:18
  70.6 2.6 %fusion.19 = f32[256,256]{0,1:T(8,128)} fusion(f32[2048,256]{0,1:T(8,128)S(1)} %copy-done.1), kind=kOutput, calls=%fused_computation.46 | convolution fusion | flops 1610612736 | bytes 2359296 | tf_op jit(solution)/shard_map/dot_general | solution.py:8
  73.1 2.5 %fusion.20 = f32[256,128]{1,0:T(8,128)} fusion(f32[2048,256]{0,1:T(8,128)S(1)} %copy-done.1, f32[2048,128]{1,0:T(8,128)S(1)} %copy-done.3), kind=kOutput, calls=%fused_computation.47 | convolution fusion | flops 805306368 | bytes 3276800 | tf_op jit(solution)/shard_map/dot_general | solution.py:8
  75.9 4.2 %fusion.18 = f32[256,256]{1,0:T(8,128)} fusion(f32[256,2048]{1,0:T(8,128)} %param.5, f32[2048,256]{1,0:T(8,128)S(1)} %copy-done), kind=kOutput, calls=%fused_computation.45 | convolution fusion | flops 1610612736 | bytes 4456448 | tf_op jit(solution)/shard_map/dot_general | solution.py:18
  80.1 70.9 %all-reduce.7.cloned.1.call-done = (f32[256,128]{1,0:T(8,128)}, f32[256,256]{0,1:T(8,128)}, f32[256,256]{0,1:T(8,128)}, f32[256,128]{1,0:T(8,128)}) async-done(((f32[256,128]{1,0:T(8,128)}, f32[256,256]{0,1:T(8,128)}, f32[256,256]{0,1:T(8,128)}, f32[256,128]{1,0:T(8,128)}), (f32[256,128]{1,0:T(8,128)}, f32[256,256]{0,1:T(8,128)}, f32[256,256]{0,1:T(8,128)}, ...) | async-done | bytes 786448 | tf_op jit(solution)/shard_map/psum | solution.py:44
  151.0 1.1 copy.9
  152.1 1.0 fusion
  153.1 0.7 copy-done.5
  153.8 11.7 %cholesky.50 = f32[128,128]{1,0:T(8,128)S(1)} custom-call(f32[128,128]{1,0:T(8,128)S(1)} %cholesky.118), custom_call_target="Cholesky" | custom-call | tf_op jit(solution)/shard_map/jit(cholesky)/cholesky | solution.py:22
  165.6 9.8 %custom-call.16 = f32[1,128,128]{1,2,0:T(8,128)S(1)} custom-call(f32[1,128,128]{2,1,0:T(8,128)S(1)} %get-tuple-element.29), custom_call_target="InvertDiagBlocksLowerTriangular" | custom-call | tf_op jit(solution)/shard_map/jit(cholesky)/cholesky | solution.py:22
  175.4 1.0 constant_dynamic-update-slice_fusion
  176.5 1.1 convolution_subtract_fusion.3
  177.6 11.8 %cholesky.105 = f32[128,128]{1,0:T(8,128)S(1)} custom-call(f32[128,128]{1,0:T(8,128)S(1)} %convolution_subtract_fusion.3), custom_call_target="Cholesky" | custom-call | tf_op jit(solution)/shard_map/jit(cholesky)/cholesky | solution.py:22
  189.5 0.7 compare_reduce_fusion
  191.5 1.0 select_select_fusion
  192.6 5.2 %while.1 = (s32[]{:T(128)}, f32[256,256]{1,0:T(8,128)S(1)}, s32[2,2]{1,0:T(2,128)S(1)}, f32[2,128,128]{2,1,0:T(8,128)}, s32[]{:T(128)}) while((s32[]{:T(128)}, f32[256,256]{1,0:T(8,128)S(1)}, s32[2,2]{1,0:T(2,128)S(1)}, f32[2,128,128]{2,1,0:T(8,128)}, s32[]{:T(128)}) %tuple.27), condition=%wide.while_cond, body=%wide.while_body.sunk | while | flops 2 | bytes 132705 | solution.py:23
  192.6 0.6 fusion.43
  193.2 2.0 bitcast_dynamic-update-slice_fusion.2
  195.8 2.0 bitcast_dynamic-update-slice_fusion.2
  197.8 20.5 %custom-call.17 = f32[2,128,128]{1,2,0:T(8,128)S(1)} custom-call(f32[2,128,128]{2,1,0:T(8,128)} %get-tuple-element.11), custom_call_target="InvertDiagBlocksLowerTriangular" | custom-call | tf_op jit(solution)/shard_map/triangular_solve | solution.py:23
  218.3 1.3 fusion.5
  219.6 1.0 convolution_subtract_fusion.2
  221.6 1.5 fusion.4
  223.2 1.3 dynamic-slice_subtract_fusion
  224.5 0.7 pad_maximum_fusion
  225.2 4.5 %convolution_subtract_fusion = f32[2048,128]{1,0:T(8,128)} fusion(f32[2048,128]{1,0:T(8,128)S(1)} %copy-done.3, f32[2048,256]{0,1:T(8,128)S(1)} %copy-done.2, f32[128,128]{1,0:T(8,128)S(1)} %fusion.11, f32[128,128]{1,0:T(8,128)S(1)} %fusion.10), kind=kOutput, calls=%fused_computation.3 | convolution fusion | flops 805601280 | bytes 4325376 | tf_op jit(solution)/shard_map/dot_general | solution.py:18
  (30 shorter events, 2.1 us)
Async XLA Ops:
  7.2 1.6 copy-start
  7.2 58.4 %all-reduce.5.cloned.1.call-start = ((), (), s32[]{:S(2)}) async-start(), calls=%async_computation.2 | async-start | bytes 4194304 | tf_op jit(solution)/shard_map/psum | solution.py:43
  11.4 1.2 copy-start.3
  11.4 139.7 %all-reduce.7.cloned.1.call-start = ((), (), s32[]{:S(2)}) async-start(), calls=%async_computation.3 | async-start | bytes 1572864 | tf_op jit(solution)/shard_map/psum | solution.py:44
  65.6 5.0 %copy-start.1 = (f32[2048,256]{0,1:T(8,128)S(1)}, f32[2048,256]{0,1:T(8,128)}, u32[]{:S(2)}) copy-start(f32[2048,256]{0,1:T(8,128)} %all-reduce.5.cloned.1.call-done) | copy-start | bytes 6291460
  75.7 154.1 %reduce-scatter.2.cloned.1.call-start = ((), (), s32[]{:S(2)}) async-start(), calls=%async_computation.1 | async-start | bytes 294912 | tf_op jit(solution)/shard_map/reduce_scatter | solution.py:38
  153.1 0.7 copy-start.5
  189.5 2.0 copy-start.4
  218.3 6.9 %copy-start.2 = (f32[2048,256]{0,1:T(8,128)S(1)}, f32[2048,256]{0,1:T(8,128)}, u32[]{:S(2)}) copy-start(f32[2048,256]{0,1:T(8,128)} %all-reduce.5.cloned.1.call-done) | copy-start | bytes 6291460
Sparse Core Ops, SparseCore 0:
  11.5 54.0 all-reduce.4
  75.8 75.2 all-reduce.6
  155.0 60.6 reduce-scatter.1
where the time goes:
time: 237 us; the launch traced here: 236 us
  waiting for transfers between devices  120 us (51%)
  other arithmetic  59.4 us (25%)
  matrix products  32.3 us (14%)
  between operations  15.2 us (6%)
  local copies, waits for them, and re-layouts  8.99 us (4%)
    psum x1, waiting for transfers between devices, shards(): lax.psum((inner_rows(panel_block, panel_block), inner_rows(panel_block, t...  70.9 us
    psum x1, waiting for transfers between devices, shards(): panel_block = lax.psum(product(matrix, selector), 'cols')  49 us
    another operation x6, other arithmetic, factor_parts(): chol_factor = jnp.linalg.cholesky(gram_matrix)  34.1 us
    another operation x4, other arithmetic, factor_parts(): lax.linalg.triangular_solve(chol_factor, cross_terms, left_side=True, low...  22.1 us
    dot_general x6, matrix products, product(): jnp.dot(left, right, precision=lax.Precision.HIGHEST, preferred_element_t...  21.9 us
    another operation x6, local copies, waits for them, and re-layouts  5.23 us
    dot_general x2, matrix products, inner_rows(): lax.dot_general(left, right, (((0,), (0,)), ((), ())), precision=lax.Prec...  5.05 us
  transfers between devices with their start and end apart: 3, of which 2 were waited for; matrix products, arithmetic and copies ran while one was open for 36% of the time, Pallas kernels for 0%

commit v1 on v0

v1 whole, which is shorter than its diff:
```python
import functools

import jax
import jax.numpy as jnp
from jax import lax
from jax.experimental import pallas as pl
from jax.experimental.pallas import tpu as pltpu
from jax.sharding import PartitionSpec as P

MESH = pl.DeviceIdType.MESH
MOST = 64
PARTS = 4
F32 = jnp.float32
BF16 = jnp.bfloat16
NN = (((1,), (0,)), ((), ()))
NT = (((1,), (1,)), ((), ()))
TN = (((0,), (0,)), ((), ()))


def split(values):
    high = values.astype(BF16)
    return high, (values - high.astype(F32)).astype(BF16)


def dot(left, right, dims=NN):
    return lax.dot_general(left, right, dims, preferred_element_type=F32)


def dot3(left, right, dims=NN):
    return dot(left[0], right[0], dims) + (dot(left[0], right[1], dims) + dot(left[1], right[0], dims))


def full_dot(left, right, dims=NN):
    return lax.dot_general(left, right, dims, precision=lax.Precision.HIGHEST, preferred_element_type=F32)


def gather_and_sum(R, C, mat, gau, piv, trl, sketch_o, gtrail_o, gpan_o, sums_o, phi_o, plo_o,
                   gath, part1, part2, in1, in2, full, gpbuf,
                   g_send, g_recv, y_send, y_recv, f_send, f_recv, s1_send, s1_recv, s2_send, s2_recv,
                   a_send, a_recv, p_send, p_recv):
    r, c = lax.axis_index("rows"), lax.axis_index("cols")
    cols_dev, panel = mat.shape[1], piv.shape[1]
    share = gau.shape[0] // R
    psh = panel // R
    ny = C // 2
    y, k = c // 2, c % 2
    partner = c + 1 - 2 * k

    barrier = pltpu.get_barrier_semaphore()
    for d in range(1, C):
        pl.semaphore_signal(barrier, inc=1, device_id=(r, lax.rem(c + d, C)), device_id_type=MESH)
    for d in range(1, R):
        pl.semaphore_signal(barrier, inc=1, device_id=(lax.rem(r + d, R), c), device_id_type=MESH)

    prow = jnp.broadcast_to(piv[...], (panel, panel))
    pcol = jnp.transpose(prow.astype(F32)).astype(jnp.int32)
    brow = jnp.zeros_like(prow)
    bcol = jnp.zeros_like(prow)
    for b in range(1, C):
        brow += (prow >= b * cols_dev).astype(jnp.int32)
        bcol += (pcol >= b * cols_dev).astype(jnp.int32)
    sub = lax.broadcasted_iota(jnp.int32, (panel, panel), 0)
    lane = lax.broadcasted_iota(jnp.int32, (panel, panel), 1)
    same = brow == bcol
    rank_row = jnp.sum(jnp.where(same & (sub < lane), 1.0, 0.0), axis=0, keepdims=True)
    rank_col = jnp.sum(jnp.where(same & (lane < sub), 1.0, 0.0), axis=1, keepdims=True)
    slot_row = brow[:1, :] * MOST + rank_row.astype(jnp.int32)
    slot_col = bcol[:, :1] * MOST + rank_col.astype(jnp.int32)
    e1 = (slot_row - c * MOST == lax.broadcasted_iota(jnp.int32, (MOST, panel), 0)).astype(F32).astype(BF16)
    e2 = (pcol[:, :1] - c * cols_dev == lax.broadcasted_iota(jnp.int32, (panel, cols_dev), 1)).astype(F32).astype(BF16)
    sel = dot(e1, e2).astype(BF16)
    m2 = split(mat[...])
    gath[c] = dot(sel, m2[0], NT) + dot(sel, m2[1], NT)

    pl.semaphore_wait(barrier, C - 1 + R - 1)

    def block_copy(source, q, target, send, recv):
        piece = gath.at[source, pl.ds(q * (MOST // PARTS), MOST // PARTS)]
        return pltpu.make_async_remote_copy(piece, piece, send, recv, device_id=(r, target), device_id_type=MESH)

    waits = []
    across = {}
    for q in range(PARTS):
        for d in range(1, ny):
            cp = block_copy(c, q, lax.rem(y + d, ny) * 2 + k, y_send.at[d - 1, q], y_recv.at[d - 1, q])
            cp.start()
            across[d, q] = cp
    for q in range(PARTS):
        cp = block_copy(c, q, partner, g_send.at[q], g_recv.at[q])
        cp.start()
        waits.append(cp)

    g2 = split(gau[...])
    t2 = split(trl[...])
    part1[:, :cols_dev] = dot3(g2, m2)
    part1[:, cols_dev:] = dot3(g2, t2)

    def scatter(part, into, rows, send, recv):
        out = []
        for d in range(1, R):
            p = lax.rem(r + d, R)
            cp = pltpu.make_async_remote_copy(
                part.at[pl.ds(pl.multiple_of(p * rows, 8), rows)], into.at[d - 1], send.at[d - 1], recv.at[d - 1],
                device_id=(p, c), device_id_type=MESH)
            cp.start()
            out.append(cp)
        return out

    first = scatter(part1, in1, share, s1_send, s1_recv)

    relays = []
    for q in range(PARTS):
        for d in range(1, ny):
            across[d, q].wait_recv()
            source = lax.rem(y + ny - d, ny) * 2 + k
            cp = block_copy(source, q, partner, f_send.at[d - 1, q], f_recv.at[d - 1, q])
            cp.start()
            relays.append(cp)
    for cp in waits:
        cp.wait_recv()
    for cp in relays:
        cp.wait_recv()

    place = (slot_col == lax.broadcasted_iota(jnp.int32, (panel, C * MOST), 1)).astype(F32).astype(BF16)
    got = split(gath[...].reshape(C * MOST, gath.shape[2]))
    high = dot(place, got[0])
    low = dot(place, got[1])
    p2 = (high.astype(BF16), low.astype(BF16))
    hl = dot(p2[0], p2[1], NT)
    part2[:, :panel] = dot(p2[0], p2[0], NT) + (hl + jnp.transpose(hl))
    part2[:, panel:] = dot3(p2, t2)
    second = scatter(part2, in2, psh, s2_send, s2_recv)

    phi_o[...] = jnp.transpose(high).astype(BF16)
    plo_o[...] = jnp.transpose(low).astype(BF16)

    for cp in first:
        cp.wait_recv()
    total = part1[pl.ds(pl.multiple_of(r * share, 8), share)]
    for d in range(1, R):
        total += in1[d - 1]
    sketch_o[...] = total[:, :cols_dev]
    gtrail_o[...] = total[:, cols_dev:]
    e3 = (prow[:1, :] - c * cols_dev == lax.broadcasted_iota(jnp.int32, (cols_dev, panel), 0)).astype(F32)
    gpbuf[0] = full_dot(total[:, :cols_dev], e3)
    third = []
    for d in range(1, C):
        cp = pltpu.make_async_remote_copy(
            gpbuf.at[0], gpbuf.at[d], p_send.at[d - 1], p_recv.at[d - 1],
            device_id=(r, lax.rem(c + d, C)), device_id_type=MESH)
        cp.start()
        third.append(cp)

    for cp in second:
        cp.wait_recv()
    mine = pl.ds(pl.multiple_of(r * psh, 8), psh)
    total2 = part2[mine]
    for d in range(1, R):
        total2 += in2[d - 1]
    full[mine] = total2
    fourth = []
    for d in range(1, R):
        cp = pltpu.make_async_remote_copy(
            full.at[mine], full.at[mine], a_send.at[d - 1], a_recv.at[d - 1],
            device_id=(lax.rem(r + d, R), c), device_id_type=MESH)
        cp.start()
        fourth.append(cp)

    for cp in third:
        cp.wait_recv()
    gp = gpbuf[0]
    for d in range(1, C):
        gp += gpbuf[d]
    gpan_o[...] = gp
    for cp in fourth:
        cp.wait_recv()
    sums_o[...] = full[...]
    for cp in list(across.values()) + waits + relays + first + second + third + fourth:
        cp.wait_send()


def factor_inverse(a):
    n = a.shape[0]
    rows = lax.broadcasted_iota(jnp.int32, (8, n), 0)
    lanes = lax.broadcasted_iota(jnp.int32, (8, n), 1)
    left = [a[8 * b:8 * b + 8, :] for b in range(n // 8)]
    right = [jnp.where(lanes == rows + 8 * b, 1.0, 0.0) for b in range(n // 8)]
    for j in range(n):
        b0, s = j // 8, j % 8
        row = left[b0][s:s + 1, :]
        scale = 1.0 / row[:, j:j + 1]
        lrow = row * scale
        rrow = right[b0][s:s + 1, :] * scale
        for b in range(b0, n // 8):
            col = jnp.broadcast_to(left[b][:, j:j + 1], (8, n))
            if b == b0:
                col = jnp.where(rows > s, col, 0.0)
            left[b] = left[b] - col * lrow
            right[b] = right[b] - col * rrow
    out = []
    for b in range(n // 8):
        diag = jnp.sum(jnp.where(lanes == rows + 8 * b, left[b], 0.0), axis=1, keepdims=True)
        out.append(right[b] * lax.rsqrt(diag))
    return jnp.concatenate(out, axis=0)


def solve_and_project(sums, gtrail, gpan, phi, plo, trl, coupling_o, projected_o, tsk_o, hbuf, lbuf, tbuf, sems):
    copies = [pltpu.make_async_copy(a, b, sems.at[i])
              for i, (a, b) in enumerate(((phi, hbuf), (plo, lbuf), (trl, tbuf)))]
    for cp in copies:
        cp.start()
    n = sums.shape[0]
    h = n // 2
    c1, c2 = sums[:h, n:], sums[h:, n:]
    i1 = factor_inverse(sums[:h, :h])
    l21 = full_dot(sums[h:, :h], i1, NT)
    k1 = full_dot(i1, c1)
    i2 = factor_inverse(sums[h:, h:n] - full_dot(l21, l21, NT))
    k2 = full_dot(i2, c2 - full_dot(l21, k1))
    coupling_o[:h, :] = k1
    coupling_o[h:, :] = k2
    w2 = full_dot(jnp.transpose(i2), k2)
    w1 = full_dot(jnp.transpose(i1), k1 - full_dot(jnp.transpose(l21), w2))
    weights = jnp.concatenate([w1, w2], axis=0)
    tsk_o[...] = gtrail[...] - full_dot(gpan[...], weights)
    w = split(weights)
    for cp in copies:
        cp.wait()
    projected_o[...] = tbuf[...] - dot3((hbuf[...], lbuf[...]), w)


def shards(R, C, matrix, gaussian, pivots, trailing):
    depth, cols_dev = matrix.shape
    sketch_rows = gaussian.shape[0]
    panel = pivots.shape[0]
    slab = trailing.shape[1]
    share, psh = sketch_rows // R, panel // R
    ny = max(C // 2 - 1, 1)
    vm = pl.BlockSpec(memory_space=pltpu.VMEM)
    anywhere = pl.BlockSpec(memory_space=pl.ANY)
    dma = pltpu.SemaphoreType.DMA
    sketch, gtrail, gpan, sums, phi, plo = pl.pallas_call(
        functools.partial(gather_and_sum, R, C),
        out_shape=[
            jax.ShapeDtypeStruct((share, cols_dev), F32),
            jax.ShapeDtypeStruct((share, slab), F32),
            jax.ShapeDtypeStruct((share, panel), F32),
            jax.ShapeDtypeStruct((panel, panel + slab), F32),
            jax.ShapeDtypeStruct((depth, panel), BF16),
            jax.ShapeDtypeStruct((depth, panel), BF16),
        ],
        in_specs=[vm] * 4,
        out_specs=[vm] * 6,
        scratch_shapes=[
            pltpu.VMEM((C, MOST, depth), F32),
            pltpu.VMEM((sketch_rows, cols_dev + slab), F32),
            pltpu.VMEM((panel, panel + slab), F32),
            pltpu.VMEM((R - 1, share, cols_dev + slab), F32),
            pltpu.VMEM((R - 1, psh, panel + slab), F32),
            pltpu.VMEM((panel, panel + slab), F32),
            pltpu.VMEM((C, share, panel), F32),
            dma((PARTS,)), dma((PARTS,)),
            dma((ny, PARTS)), dma((ny, PARTS)),
            dma((ny, PARTS)), dma((ny, PARTS)),
            dma((R - 1,)), dma((R - 1,)),
            dma((R - 1,)), dma((R - 1,)),
            dma((R - 1,)), dma((R - 1,)),
            dma((C - 1,)), dma((C - 1,)),
        ],
        compiler_params=pltpu.CompilerParams(
            collective_id=0, has_side_effects=True, vmem_limit_bytes=56 * 1024 * 1024),
    )(matrix, gaussian, pivots.reshape(1, panel), trailing)
    coupling, projected, tsk = pl.pallas_call(
        solve_and_project,
        out_shape=[
            jax.ShapeDtypeStruct((panel, slab), F32),
            jax.ShapeDtypeStruct((depth, slab), F32),
            jax.ShapeDtypeStruct((share, slab), F32),
        ],
        in_specs=[vm] * 3 + [anywhere] * 3,
        out_specs=[vm] * 3,
        scratch_shapes=[
            pltpu.VMEM((depth, panel), BF16),
            pltpu.VMEM((depth, panel), BF16),
            pltpu.VMEM((depth, slab), F32),
            dma((3,)),
        ],
        compiler_params=pltpu.CompilerParams(vmem_limit_bytes=56 * 1024 * 1024),
    )(sums, gtrail, gpan, phi, plo, trailing)
    return sketch, coupling, projected, tsk


def solution(mesh):
    placed = (P("rows", "cols"), P(None, "rows"), P(), P("rows", "cols"))
    return jax.shard_map(
        functools.partial(shards, mesh.shape["rows"], mesh.shape["cols"]),
        mesh=mesh,
        in_specs=placed,
        out_specs=(P("rows", "cols"), P(None, "cols"), P("rows", "cols"), P("rows", "cols")),
        check_vma=False,
    )
```

time: 237 us -> 72.2 us (0.30)
  the two profiles are of different devices: /device:TPU:0 before, /device:TPU:24 now
where the time goes in v1:
time: 72.2 us; the launch traced here: 72 us
  Pallas kernels  70.8 us (98%)
    pallas_call x1, Pallas kernels, shards(): pl.pallas_call(functools.partial(gather_and_sum, R, C), out_shape=[jax.Sh...  44.3 us
    pallas_call x1, Pallas kernels, shards(): pl.pallas_call(solve_and_project, out_shape=[jax.ShapeDtypeStruct((panel,...  26.5 us

profile of v1, /device:TPU:24, one launch (start us, length us, event | category | flops | bytes accessed | tf_op | source)
XLA Modules:
  0.0 72.0 jit_solution(7596862715540316376)
XLA Ops:
  0.6 44.3 %shard_map.75 = (f32[32,256]{1,0:T(8,128)}, f32[32,128]{1,0:T(8,128)}, f32[32,256]{1,0:T(8,128)}, f32[256,384]{1,0:T(8,128)}, bf16[2048,256]{1,0:T(8,128)(2,1)}, /*index=5*/bf16[2048,256]{1,0:T(8,128)(2,1)}) custom-call(f32[2048,256]{1,0:T(8,128)} %mat.1, f32[256,2048]{1,0:T(8,128)} %gau.1, s32[1,256]{1,0:T(1,128)} %bitcast.1, f32[2048,128]{1,0:T(8,128)} %trl.3), custom_call_target="tpu_custom_call" | custom-call | tf_op jit(solution)/shard_map/pallas_call | solution.py:242
  44.9 0.0 copy-start
  44.9 26.5 %shard_map.76 = (f32[256,128]{1,0:T(8,128)}, f32[2048,128]{1,0:T(8,128)}, f32[32,128]{1,0:T(8,128)}) custom-call(f32[256,384]{1,0:T(8,128)} %get-tuple-element.14.sums, f32[32,128]{1,0:T(8,128)} %get-tuple-element.15.gtrail, f32[32,256]{1,0:T(8,128)} %get-tuple-element.16.gpan, bf16[2048,256]{1,0:T(8,128)(2,1)} %get-tuple-element.17.phi, ...), custom_call_target="tpu_custom_call" | custom-call | tf_op jit(solution)/shard_map/pallas_call | solution.py:273
  71.4 0.0 copy-done
  71.4 0.6 copy.9
Async XLA Ops:
  44.9 26.5 %copy-start = (f32[32,256]{1,0:T(8,128)S(1)}, f32[32,256]{1,0:T(8,128)}, u32[]{:S(2)}) copy-start(f32[32,256]{1,0:T(8,128)} %get-tuple-element.26) | copy-start | bytes 98308

commit v2 on v1

--- a/solution.py
+++ b/solution.py
@@ -185,22 +185,35 @@
     lanes = lax.broadcasted_iota(jnp.int32, (8, n), 1)
     left = [a[8 * b:8 * b + 8, :] for b in range(n // 8)]
     right = [jnp.where(lanes == rows + 8 * b, 1.0, 0.0) for b in range(n // 8)]
-    for j in range(n):
-        b0, s = j // 8, j % 8
-        row = left[b0][s:s + 1, :]
-        scale = 1.0 / row[:, j:j + 1]
-        lrow = row * scale
-        rrow = right[b0][s:s + 1, :] * scale
-        for b in range(b0, n // 8):
-            col = jnp.broadcast_to(left[b][:, j:j + 1], (8, n))
-            if b == b0:
-                col = jnp.where(rows > s, col, 0.0)
-            left[b] = left[b] - col * lrow
-            right[b] = right[b] - col * rrow
     out = []
-    for b in range(n // 8):
-        diag = jnp.sum(jnp.where(lanes == rows + 8 * b, left[b], 0.0), axis=1, keepdims=True)
-        out.append(right[b] * lax.rsqrt(diag))
+    for b0 in range(n // 8):
+        x, y = left[b0], right[b0]
+        cols = [jnp.broadcast_to(x[:, 8 * b0 + i:8 * b0 + i + 1], (8, n)) for i in range(8)]
+        done = []
+        for s in range(0, 8, 2):
+            c0, c1 = cols[s], cols[s + 1]
+            p, q, t = c0[s:s + 1], c0[s + 1:s + 2], c1[s + 1:s + 2]
+            det = p * t - q * q
+            inv = 1.0 / det
+            ip, iq, it = t * inv, -q * inv, p * inv
+            y0, y1 = y[s:s + 1], y[s + 1:s + 2]
+            done.append(y0 * lax.rsqrt(p))
+            done.append((y1 - (q / p) * y0) * lax.rsqrt(det / p))
+
+            def eliminate(block):
+                r0, r1 = block[s:s + 1], block[s + 1:s + 2]
+                u0, u1 = ip * r0 + iq * r1, iq * r0 + it * r1
+                return jnp.where(rows == s, u0, jnp.where(rows == s + 1, u1, block - c0 * u0 - c1 * u1))
+
+            for i in range(s + 2, 8):
+                cols[i] = eliminate(cols[i])
+            x, y = eliminate(x), eliminate(y)
+        out.append(jnp.concatenate(done, axis=0))
+        for b in range(b0 + 1, n // 8):
+            across = [jnp.broadcast_to(left[b][:, 8 * b0 + i:8 * b0 + i + 1], (8, n)) for i in range(8)]
+            for i in range(8):
+                left[b] = left[b] - across[i] * x[i:i + 1]
+                right[b] = right[b] - across[i] * y[i:i + 1]
     return jnp.concatenate(out, axis=0)
 
 

time: 72.2 us -> 57.5 us (0.80)
  Pallas kernels: 70.8 us -> 56 us
    pallas_call x1, Pallas kernels: 26.5 us -> 11.8 us  [shards(): pl.pallas_call(solve_and_project, out_shape=[jax.ShapeDtypeStruct((panel,...]
where the time goes in v2:
time: 57.5 us; the launch traced here: 57.3 us
  Pallas kernels  56 us (97%)
  between operations  0.66 us (1%)
  local copies, waits for them, and re-layouts  0.62 us (1%)
    pallas_call x1, Pallas kernels, shards(): pl.pallas_call(functools.partial(gather_and_sum, R, C), out_shape=[jax.Sh...  44.3 us
    pallas_call x1, Pallas kernels, shards(): pl.pallas_call(solve_and_project, out_shape=[jax.ShapeDtypeStruct((panel,...  11.8 us

profile of v2, /device:TPU:24, one launch (start us, length us, event | category | flops | bytes accessed | tf_op | source)
XLA Modules:
  0.0 57.3 jit_solution(11206277673622312702)
XLA Ops:
  0.6 44.3 %shard_map.75 = (f32[32,256]{1,0:T(8,128)}, f32[32,128]{1,0:T(8,128)}, f32[32,256]{1,0:T(8,128)}, f32[256,384]{1,0:T(8,128)}, bf16[2048,256]{1,0:T(8,128)(2,1)}, /*index=5*/bf16[2048,256]{1,0:T(8,128)(2,1)}) custom-call(f32[2048,256]{1,0:T(8,128)} %mat.1, f32[256,2048]{1,0:T(8,128)} %gau.1, s32[1,256]{1,0:T(1,128)} %bitcast.1, f32[2048,128]{1,0:T(8,128)} %trl.3), custom_call_target="tpu_custom_call" | custom-call | tf_op jit(solution)/shard_map/pallas_call | solution.py:255
  44.9 0.0 copy-start
  44.9 11.8 %shard_map.76 = (f32[256,128]{1,0:T(8,128)}, f32[2048,128]{1,0:T(8,128)}, f32[32,128]{1,0:T(8,128)}) custom-call(f32[256,384]{1,0:T(8,128)} %get-tuple-element.14.sums, f32[32,128]{1,0:T(8,128)} %get-tuple-element.15.gtrail, f32[32,256]{1,0:T(8,128)} %get-tuple-element.16.gpan, bf16[2048,256]{1,0:T(8,128)(2,1)} %get-tuple-element.17.phi, ...), custom_call_target="tpu_custom_call" | custom-call | tf_op jit(solution)/shard_map/pallas_call | solution.py:286
  56.7 0.0 copy-done
  56.7 0.6 %copy.9 = f32[32,256]{1,0:T(8,128)} copy(f32[32,256]{1,0:T(8,128)S(1)} %copy-done) | data formatting | bytes 65536
Async XLA Ops:
  44.9 11.8 %copy-start = (f32[32,256]{1,0:T(8,128)S(1)}, f32[32,256]{1,0:T(8,128)}, u32[]{:S(2)}) copy-start(f32[32,256]{1,0:T(8,128)} %get-tuple-element.26) | copy-start | bytes 98308

commit v3 on v2

--- a/solution.py
+++ b/solution.py
@@ -176,6 +176,180 @@
         cp.wait_recv()
     sums_o[...] = full[...]
     for cp in list(across.values()) + waits + relays + first + second + third + fourth:
+        cp.wait_send()
+
+
+def ordered(place, values):
+    high = values.astype(BF16)
+    rest = values - high.astype(F32)
+    mid = rest.astype(BF16)
+    low = (rest - mid.astype(F32)).astype(BF16)
+    return (dot(place, low) + dot(place, mid)) + dot(place, high)
+
+
+def gather_by_halves(R, C, mat, gau_in, piv, trl_in, sketch_o, gtrail_o, gpan_o, sums_o, phi_o, plo_o, place_o,
+                     gau, trl, gath, part1, near, far, in1, in_near, in_far, full_near, full_far, diag, gpbuf,
+                     l_sem, g_send, g_recv, y_send, y_recv, f_send, f_recv, s_send, s_recv, n_send, n_recv,
+                     o_send, o_recv, an_send, an_recv, ao_send, ao_recv, p_send, p_recv, d_send, d_recv):
+    r, c = lax.axis_index("rows"), lax.axis_index("cols")
+    cols_dev, panel = mat.shape[1], piv.shape[1]
+    depth = mat.shape[0]
+    share = gau.shape[0] // R
+    half = panel // 2
+    hsh = half // R
+    y, k = c // 2, c % 2
+    partner = c + 1 - 2 * k
+    opposite = lax.rem(c + 2, C)
+
+    loads = [pltpu.make_async_copy(trl_in, trl, l_sem.at[0]), pltpu.make_async_copy(gau_in, gau, l_sem.at[1])]
+    for cp in loads:
+        cp.start()
+    barrier = pltpu.get_barrier_semaphore()
+    for d in range(1, C):
+        pl.semaphore_signal(barrier, inc=1, device_id=(r, lax.rem(c + d, C)), device_id_type=MESH)
+    for d in range(1, R):
+        pl.semaphore_signal(barrier, inc=1, device_id=(lax.rem(r + d, R), c), device_id_type=MESH)
+
+    prow = jnp.broadcast_to(piv[...], (panel, panel))
+    pcol = jnp.transpose(prow.astype(F32)).astype(jnp.int32)
+    brow = jnp.zeros_like(prow)
+    bcol = jnp.zeros_like(prow)
+    for b in range(1, C):
+        brow += (prow >= b * cols_dev).astype(jnp.int32)
+        bcol += (pcol >= b * cols_dev).astype(jnp.int32)
+    sub = lax.broadcasted_iota(jnp.int32, (panel, panel), 0)
+    lane = lax.broadcasted_iota(jnp.int32, (panel, panel), 1)
+    same = brow == bcol
+    rank_row = jnp.sum(jnp.where(same & (sub < lane), 1.0, 0.0), axis=0, keepdims=True)
+    rank_col = jnp.sum(jnp.where(same & (lane < sub), 1.0, 0.0), axis=1, keepdims=True)
+    slot_row = brow[:1, :] * MOST + rank_row.astype(jnp.int32)
+    slot_col = bcol[:, :1] * MOST + rank_col.astype(jnp.int32)
+    e1 = (slot_row - c * MOST == lax.broadcasted_iota(jnp.int32, (MOST, panel), 0)).astype(F32).astype(BF16)
+    e2 = (pcol[:, :1] - c * cols_dev == lax.broadcasted_iota(jnp.int32, (panel, cols_dev), 1)).astype(F32).astype(BF16)
+    sel = dot(e1, e2).astype(BF16)
+    m2 = split(mat[...])
+    gath[c] = dot(sel, m2[0], NT) + dot(sel, m2[1], NT)
+
+    pl.semaphore_wait(barrier, C - 1 + R - 1)
+
+    def block_copy(source, q, target, send, recv):
+        piece = gath.at[source, pl.ds(q * (MOST // PARTS), MOST // PARTS)]
+        return pltpu.make_async_remote_copy(piece, piece, send, recv, device_id=(r, target), device_id_type=MESH)
+
+    def scatter(part, into, rows, send, recv):
+        out = []
+        for d in range(1, R):
+            p = lax.rem(r + d, R)
+            cp = pltpu.make_async_remote_copy(
+                part.at[pl.ds(pl.multiple_of(p * rows, 8), rows)], into.at[d - 1], send.at[d - 1], recv.at[d - 1],
+                device_id=(p, c), device_id_type=MESH)
+            cp.start()
+            out.append(cp)
+        return out
+
+    def finish(copies, part, into, rows):
+        for cp in copies:
+            cp.wait_recv()
+        total = part[pl.ds(pl.multiple_of(r * rows, 8), rows)]
+        for d in range(1, R):
+            total += into[d - 1]
+        return total
+
+    def spread(total, whole, rows, send, recv):
+        mine = pl.ds(pl.multiple_of(r * rows, 8), rows)
+        whole[mine] = total
+        out = []
+        for d in range(1, R):
+            cp = pltpu.make_async_remote_copy(
+                whole.at[mine], whole.at[mine], send.at[d - 1], recv.at[d - 1],
+                device_id=(lax.rem(r + d, R), c), device_id_type=MESH)
+            cp.start()
+            out.append(cp)
+        return out
+
+    across = [block_copy(c, q, opposite, y_send.at[q], y_recv.at[q]) for q in range(PARTS)]
+    beside = [block_copy(c, q, partner, g_send.at[q], g_recv.at[q]) for q in range(PARTS)]
+    relays = [block_copy(opposite, q, partner, f_send.at[q], f_recv.at[q]) for q in range(PARTS)]
+    for cp in across + beside:
+        cp.start()
+
+    loads[0].wait()
+    t2 = split(trl[...])
+    for cp in beside:
+        cp.wait_recv()
+    own = gath[pl.ds(2 * y, 2)].reshape(half, depth)
+    o2 = split(own)
+    near[:, :half] = dot3(o2, o2, NT)
+    near[:, half:] = dot3(o2, t2)
+    near_out = scatter(near, in_near, hsh, n_send, n_recv)
+
+    loads[1].wait()
+    g2 = split(gau[...])
+    part1[:, :cols_dev] = dot3(g2, m2)
+    part1[:, cols_dev:] = dot3(g2, t2)
+    sketch_out = scatter(part1, in1, share, s_send, s_recv)
+
+    near_all = spread(finish(near_out, near, in_near, hsh), full_near, hsh, an_send, an_recv)
+    for q in range(PARTS):
+        across[q].wait_recv()
+        relays[q].start()
+    own_t = jnp.transpose(own)
+    t_high, t_low = split(own_t)
+    phi_o[:, :half] = t_high
+    plo_o[:, :half] = t_low
+    for cp in near_all:
+        cp.wait_recv()
+    swap = pltpu.make_async_remote_copy(
+        full_near.at[:, pl.ds(0, half)], diag, d_send.at[0], d_recv.at[0],
+        device_id=(r, opposite), device_id_type=MESH)
+    swap.start()
+    for cp in relays:
+        cp.wait_recv()
+
+    other = gath[pl.ds(2 * (1 - y), 2)].reshape(half, depth)
+    r2 = split(other)
+    far[:, :half] = dot3(r2, o2, NT)
+    far[:, half:] = dot3(r2, t2)
+    far_out = scatter(far, in_far, hsh, o_send, o_recv)
+
+    r_high, r_low = split(jnp.transpose(other))
+    phi_o[:, half:] = r_high
+    plo_o[:, half:] = r_low
+    slot = lane + half * y
+    slot = jnp.where(slot >= panel, slot - panel, slot)
+    place = (slot_col == slot).astype(F32).astype(BF16)
+    place_o[...] = place
+
+    far_all = spread(finish(far_out, far, in_far, hsh), full_far, hsh, ao_send, ao_recv)
+
+    total = finish(sketch_out, part1, in1, share)
+    sketch_o[...] = total[:, :cols_dev]
+    gtrail_o[...] = total[:, cols_dev:]
+    e3 = (prow[:1, :] - c * cols_dev == lax.broadcasted_iota(jnp.int32, (cols_dev, panel), 0)).astype(F32)
+    gpbuf[0] = full_dot(total[:, :cols_dev], e3)
+    third = []
+    for d in range(1, C):
+        cp = pltpu.make_async_remote_copy(
+            gpbuf.at[0], gpbuf.at[d], p_send.at[d - 1], p_recv.at[d - 1],
+            device_id=(r, lax.rem(c + d, C)), device_id_type=MESH)
+        cp.start()
+        third.append(cp)
+    swap.wait_recv()
+    for cp in far_all:
+        cp.wait_recv()
+    mixed = full_far[:, :half]
+    first_rows = jnp.concatenate([full_near[:, :half], jnp.transpose(mixed), full_near[:, half:]], axis=1)
+    last_rows = jnp.concatenate([mixed, diag[...], full_far[:, half:]], axis=1)
+    by_rows = ordered(place, jnp.concatenate([first_rows, last_rows], axis=0))
+    sums_o[:, panel:] = by_rows[:, panel:]
+    sums_o[:, :panel] = ordered(place, jnp.transpose(by_rows[:, :panel]))
+    for cp in third:
+        cp.wait_recv()
+    gp = gpbuf[0]
+    for d in range(1, C):
+        gp += gpbuf[d]
+    gpan_o[...] = gp
+    for cp in across + beside + relays + near_out + sketch_out + near_all + far_out + far_all + third + [swap]:
         cp.wait_send()
 
 
@@ -217,7 +391,7 @@
     return jnp.concatenate(out, axis=0)
 
 
-def solve_and_project(sums, gtrail, gpan, phi, plo, trl, coupling_o, projected_o, tsk_o, hbuf, lbuf, tbuf, sems):
+def solve_and_project(sums, gtrail, gpan, place, phi, plo, trl, coupling_o, projected_o, tsk_o, hbuf, lbuf, tbuf, sems):
     copies = [pltpu.make_async_copy(a, b, sems.at[i])
               for i, (a, b) in enumerate(((phi, hbuf), (plo, lbuf), (trl, tbuf)))]
     for cp in copies:
@@ -236,7 +410,7 @@
     w1 = full_dot(jnp.transpose(i1), k1 - full_dot(jnp.transpose(l21), w2))
     weights = jnp.concatenate([w1, w2], axis=0)
     tsk_o[...] = gtrail[...] - full_dot(gpan[...], weights)
-    w = split(weights)
+    w = tuple(dot(place[...], piece, TN).astype(BF16) for piece in split(weights))
     for cp in copies:
         cp.wait()
     projected_o[...] = tbuf[...] - dot3((hbuf[...], lbuf[...]), w)
@@ -252,37 +426,77 @@
     vm = pl.BlockSpec(memory_space=pltpu.VMEM)
     anywhere = pl.BlockSpec(memory_space=pl.ANY)
     dma = pltpu.SemaphoreType.DMA
-    sketch, gtrail, gpan, sums, phi, plo = pl.pallas_call(
-        functools.partial(gather_and_sum, R, C),
-        out_shape=[
-            jax.ShapeDtypeStruct((share, cols_dev), F32),
-            jax.ShapeDtypeStruct((share, slab), F32),
-            jax.ShapeDtypeStruct((share, panel), F32),
-            jax.ShapeDtypeStruct((panel, panel + slab), F32),
-            jax.ShapeDtypeStruct((depth, panel), BF16),
-            jax.ShapeDtypeStruct((depth, panel), BF16),
-        ],
-        in_specs=[vm] * 4,
-        out_specs=[vm] * 6,
-        scratch_shapes=[
-            pltpu.VMEM((C, MOST, depth), F32),
-            pltpu.VMEM((sketch_rows, cols_dev + slab), F32),
-            pltpu.VMEM((panel, panel + slab), F32),
-            pltpu.VMEM((R - 1, share, cols_dev + slab), F32),
-            pltpu.VMEM((R - 1, psh, panel + slab), F32),
-            pltpu.VMEM((panel, panel + slab), F32),
-            pltpu.VMEM((C, share, panel), F32),
-            dma((PARTS,)), dma((PARTS,)),
-            dma((ny, PARTS)), dma((ny, PARTS)),
-            dma((ny, PARTS)), dma((ny, PARTS)),
-            dma((R - 1,)), dma((R - 1,)),
-            dma((R - 1,)), dma((R - 1,)),
-            dma((R - 1,)), dma((R - 1,)),
-            dma((C - 1,)), dma((C - 1,)),
-        ],
-        compiler_params=pltpu.CompilerParams(
-            collective_id=0, has_side_effects=True, vmem_limit_bytes=56 * 1024 * 1024),
-    )(matrix, gaussian, pivots.reshape(1, panel), trailing)
+    if C == 4 and C * MOST == panel and panel == 2 * slab and (panel // 2) % (8 * R) == 0:
+        half = panel // 2
+        sketch, gtrail, gpan, sums, phi, plo, place = pl.pallas_call(
+            functools.partial(gather_by_halves, R, C),
+            out_shape=[
+                jax.ShapeDtypeStruct((share, cols_dev), F32),
+                jax.ShapeDtypeStruct((share, slab), F32),
+                jax.ShapeDtypeStruct((share, panel), F32),
+                jax.ShapeDtypeStruct((panel, panel + slab), F32),
+                jax.ShapeDtypeStruct((depth, panel), BF16),
+                jax.ShapeDtypeStruct((depth, panel), BF16),
+                jax.ShapeDtypeStruct((panel, panel), BF16),
+            ],
+            in_specs=[vm, anywhere, vm, anywhere],
+            out_specs=[vm] * 7,
+            scratch_shapes=[
+                pltpu.VMEM((sketch_rows, depth), F32),
+                pltpu.VMEM((depth, slab), F32),
+                pltpu.VMEM((C, MOST, depth), F32),
+                pltpu.VMEM((sketch_rows, cols_dev + slab), F32),
+                pltpu.VMEM((half, half + slab), F32),
+                pltpu.VMEM((half, half + slab), F32),
+                pltpu.VMEM((R - 1, share, cols_dev + slab), F32),
+                pltpu.VMEM((R - 1, half // R, half + slab), F32),
+                pltpu.VMEM((R - 1, half // R, half + slab), F32),
+                pltpu.VMEM((half, half + slab), F32),
+                pltpu.VMEM((half, half + slab), F32),
+                pltpu.VMEM((half, half), F32),
+                pltpu.VMEM((C, share, panel), F32),
+                dma((2,)),
+                *[dma((PARTS,))] * 6,
+                *[dma((R - 1,))] * 10,
+                *[dma((C - 1,))] * 2,
+                *[dma((1,))] * 2,
+            ],
+            compiler_params=pltpu.CompilerParams(
+                collective_id=0, has_side_effects=True, vmem_limit_bytes=56 * 1024 * 1024),
+        )(matrix, gaussian, pivots.reshape(1, panel), trailing)
+    else:
+        sketch, gtrail, gpan, sums, phi, plo = pl.pallas_call(
+            functools.partial(gather_and_sum, R, C),
+            out_shape=[
+                jax.ShapeDtypeStruct((share, cols_dev), F32),
+                jax.ShapeDtypeStruct((share, slab), F32),
+                jax.ShapeDtypeStruct((share, panel), F32),
+                jax.ShapeDtypeStruct((panel, panel + slab), F32),
+                jax.ShapeDtypeStruct((depth, panel), BF16),
+                jax.ShapeDtypeStruct((depth, panel), BF16),
+            ],
+            in_specs=[vm] * 4,
+            out_specs=[vm] * 6,
+            scratch_shapes=[
+                pltpu.VMEM((C, MOST, depth), F32),
+                pltpu.VMEM((sketch_rows, cols_dev + slab), F32),
+                pltpu.VMEM((panel, panel + slab), F32),
+                pltpu.VMEM((R - 1, share, cols_dev + slab), F32),
+                pltpu.VMEM((R - 1, psh, panel + slab), F32),
+                pltpu.VMEM((panel, panel + slab), F32),
+                pltpu.VMEM((C, share, panel), F32),
+                dma((PARTS,)), dma((PARTS,)),
+                dma((ny, PARTS)), dma((ny, PARTS)),
+                dma((ny, PARTS)), dma((ny, PARTS)),
+                dma((R - 1,)), dma((R - 1,)),
+                dma((R - 1,)), dma((R - 1,)),
+                dma((R - 1,)), dma((R - 1,)),
+                dma((C - 1,)), dma((C - 1,)),
+            ],
+            compiler_params=pltpu.CompilerParams(
+                collective_id=0, has_side_effects=True, vmem_limit_bytes=56 * 1024 * 1024),
+        )(matrix, gaussian, pivots.reshape(1, panel), trailing)
+        place = jnp.eye(panel, dtype=BF16)
     coupling, projected, tsk = pl.pallas_call(
         solve_and_project,
         out_shape=[
@@ -290,7 +504,7 @@
             jax.ShapeDtypeStruct((depth, slab), F32),
             jax.ShapeDtypeStruct((share, slab), F32),
         ],
-        in_specs=[vm] * 3 + [anywhere] * 3,
+        in_specs=[vm] * 4 + [anywhere] * 3,
         out_specs=[vm] * 3,
         scratch_shapes=[
             pltpu.VMEM((depth, panel), BF16),
@@ -299,7 +513,7 @@
             dma((3,)),
         ],
         compiler_params=pltpu.CompilerParams(vmem_limit_bytes=56 * 1024 * 1024),
-    )(sums, gtrail, gpan, phi, plo, trailing)
+    )(sums, gtrail, gpan, place, phi, plo, trailing)
     return sketch, coupling, projected, tsk
 
 

time: 57.5 us -> 52.8 us (0.918)
  the two profiles are of different devices: /device:TPU:24 before, /device:TPU:0 now
where the time goes in v3:
time: 52.8 us; the launch traced here: 52.6 us
  Pallas kernels  51.3 us (97%)
  between operations  0.66 us (1%)
  local copies, waits for them, and re-layouts  0.62 us (1%)
    pallas_call x1, Pallas kernels, shards(): pl.pallas_call(functools.partial(gather_by_halves, R, C), out_shape=[jax....  39.4 us
    pallas_call x1, Pallas kernels, shards(): pl.pallas_call(solve_and_project, out_shape=[jax.ShapeDtypeStruct((panel,...  11.9 us

profile of v3, /device:TPU:0, one launch (start us, length us, event | category | flops | bytes accessed | tf_op | source)
XLA Modules:
  0.0 52.6 jit_solution(14968855503935411113)
XLA Ops:
  0.6 39.4 %shard_map.75 = (f32[32,256]{1,0:T(8,128)}, f32[32,128]{1,0:T(8,128)}, f32[32,256]{1,0:T(8,128)}, f32[256,384]{1,0:T(8,128)}, bf16[2048,256]{1,0:T(8,128)(2,1)},...) custom-call(f32[2048,256]{1,0:T(8,128)} %mat.1, f32[256,2048]{1,0:T(8,128)} %gau_in.1, s32[1,256]{1,0:T(1,128)} %bitcast.1, ...), custom_call_target="tpu_custom_call" | custom-call | tf_op jit(solution)/shard_map/pallas_call | solution.py:431
  40.1 0.0 copy-start
  40.1 11.9 %shard_map.76 = (f32[256,128]{1,0:T(8,128)}, f32[2048,128]{1,0:T(8,128)}, f32[32,128]{1,0:T(8,128)}) custom-call(f32[256,384]{1,0:T(8,128)} %get-tuple-element.15.sums, f32[32,128]{1,0:T(8,128)} %get-tuple-element.16.gtrail, f32[32,256]{1,0:T(8,128)} %get-tuple-element.17.gpan, bf16[256,256]{1,0:T(8,128)(2,1)} %get-tuple-element.18.place, ...), custom_call_target="tpu_custom_call" | custom-call | tf_op jit(solution)/shard_map/pallas_call | solution.py:500
  52.0 0.0 copy-done
  52.0 0.6 %copy.9 = f32[32,256]{1,0:T(8,128)} copy(f32[32,256]{1,0:T(8,128)S(1)} %copy-done) | data formatting | bytes 65536
Async XLA Ops:
  40.1 11.9 %copy-start = (f32[32,256]{1,0:T(8,128)S(1)}, f32[32,256]{1,0:T(8,128)}, u32[]{:S(2)}) copy-start(f32[32,256]{1,0:T(8,128)} %get-tuple-element.28) | copy-start | bytes 98308

commit v4 on v3

--- a/solution.py
+++ b/solution.py
@@ -188,8 +188,8 @@
 
 
 def gather_by_halves(R, C, mat, gau_in, piv, trl_in, sketch_o, gtrail_o, gpan_o, sums_o, phi_o, plo_o, place_o,
-                     gau, trl, gath, part1, near, far, in1, in_near, in_far, full_near, full_far, diag, gpbuf,
-                     l_sem, g_send, g_recv, y_send, y_recv, f_send, f_recv, s_send, s_recv, n_send, n_recv,
+                     gau, trl, hbuf, lbuf, inx, pairs, gath, part1, near, far, in1, in_near, in_far, full_near, full_far, diag, gpbuf,
+                     l_sem, x_send, x_recv, g_send, g_recv, y_send, y_recv, f_send, f_recv, s_send, s_recv, n_send, n_recv,
                      o_send, o_recv, an_send, an_recv, ao_send, ao_recv, p_send, p_recv, d_send, d_recv):
     r, c = lax.axis_index("rows"), lax.axis_index("cols")
     cols_dev, panel = mat.shape[1], piv.shape[1]
@@ -287,16 +287,37 @@
     g2 = split(gau[...])
     part1[:, :cols_dev] = dot3(g2, m2)
     part1[:, cols_dev:] = dot3(g2, t2)
-    sketch_out = scatter(part1, in1, share, s_send, s_recv)
+    side = lax.rem(r, 2)
+    pair_out = []
+    for i in range(R // 2):
+        cp = pltpu.make_async_remote_copy(
+            part1.at[pl.ds(pl.multiple_of((2 * i + 1 - side) * share, 8), share)], inx.at[i], x_send.at[i], x_recv.at[i],
+            device_id=(r + 1 - 2 * side, c), device_id_type=MESH)
+        cp.start()
+        pair_out.append(cp)
 
     near_all = spread(finish(near_out, near, in_near, hsh), full_near, hsh, an_send, an_recv)
-    for q in range(PARTS):
+    across[0].wait_recv()
+    relays[0].start()
+    for cp in pair_out:
+        cp.wait_recv()
+    for i in range(R // 2):
+        pairs[i] = part1[pl.ds(pl.multiple_of((2 * i + side) * share, 8), share)] + inx[i]
+    sketch_out = []
+    for d in range(1, R // 2):
+        to = lax.rem(r // 2 + d, R // 2)
+        cp = pltpu.make_async_remote_copy(
+            pairs.at[to], in1.at[d - 1], s_send.at[d - 1], s_recv.at[d - 1],
+            device_id=(2 * to + side, c), device_id_type=MESH)
+        cp.start()
+        sketch_out.append(cp)
+    for q in range(1, PARTS):
         across[q].wait_recv()
         relays[q].start()
     own_t = jnp.transpose(own)
     t_high, t_low = split(own_t)
-    phi_o[:, :half] = t_high
-    plo_o[:, :half] = t_low
+    hbuf[:, :half] = t_high
+    lbuf[:, :half] = t_low
     for cp in near_all:
         cp.wait_recv()
     swap = pltpu.make_async_remote_copy(
@@ -313,8 +334,11 @@
     far_out = scatter(far, in_far, hsh, o_send, o_recv)
 
     r_high, r_low = split(jnp.transpose(other))
-    phi_o[:, half:] = r_high
-    plo_o[:, half:] = r_low
+    hbuf[:, half:] = r_high
+    lbuf[:, half:] = r_low
+    stores = [pltpu.make_async_copy(hbuf, phi_o, l_sem.at[2]), pltpu.make_async_copy(lbuf, plo_o, l_sem.at[3])]
+    for cp in stores:
+        cp.start()
     slot = lane + half * y
     slot = jnp.where(slot >= panel, slot - panel, slot)
     place = (slot_col == slot).astype(F32).astype(BF16)
@@ -322,7 +346,11 @@
 
     far_all = spread(finish(far_out, far, in_far, hsh), full_far, hsh, ao_send, ao_recv)
 
-    total = finish(sketch_out, part1, in1, share)
+    for cp in sketch_out:
+        cp.wait_recv()
+    total = pairs[r // 2]
+    for d in range(1, R // 2):
+        total += in1[d - 1]
     sketch_o[...] = total[:, :cols_dev]
     gtrail_o[...] = total[:, cols_dev:]
     e3 = (prow[:1, :] - c * cols_dev == lax.broadcasted_iota(jnp.int32, (cols_dev, panel), 0)).astype(F32)
@@ -349,8 +377,10 @@
     for d in range(1, C):
         gp += gpbuf[d]
     gpan_o[...] = gp
-    for cp in across + beside + relays + near_out + sketch_out + near_all + far_out + far_all + third + [swap]:
+    for cp in across + beside + relays + near_out + pair_out + sketch_out + near_all + far_out + far_all + third + [swap]:
         cp.wait_send()
+    for cp in stores:
+        cp.wait()
 
 
 def factor_inverse(a):
@@ -391,11 +421,12 @@
     return jnp.concatenate(out, axis=0)
 
 
-def solve_and_project(sums, gtrail, gpan, place, phi, plo, trl, coupling_o, projected_o, tsk_o, hbuf, lbuf, tbuf, sems):
+def solve_and_project(sums, gtrail, gpan, place, sketch, phi, plo, trl, sketch_o, coupling_o, projected_o, tsk_o, hbuf, lbuf, tbuf, sems):
     copies = [pltpu.make_async_copy(a, b, sems.at[i])
               for i, (a, b) in enumerate(((phi, hbuf), (plo, lbuf), (trl, tbuf)))]
     for cp in copies:
         cp.start()
+    sketch_o[...] = sketch[...]
     n = sums.shape[0]
     h = n // 2
     c1, c2 = sums[:h, n:], sums[h:, n:]
@@ -426,7 +457,7 @@
     vm = pl.BlockSpec(memory_space=pltpu.VMEM)
     anywhere = pl.BlockSpec(memory_space=pl.ANY)
     dma = pltpu.SemaphoreType.DMA
-    if C == 4 and C * MOST == panel and panel == 2 * slab and (panel // 2) % (8 * R) == 0:
+    if C == 4 and R % 2 == 0 and C * MOST == panel and panel == 2 * slab and (panel // 2) % (8 * R) == 0:
         half = panel // 2
         sketch, gtrail, gpan, sums, phi, plo, place = pl.pallas_call(
             functools.partial(gather_by_halves, R, C),
@@ -440,10 +471,14 @@
                 jax.ShapeDtypeStruct((panel, panel), BF16),
             ],
             in_specs=[vm, anywhere, vm, anywhere],
-            out_specs=[vm] * 7,
+            out_specs=[vm] * 4 + [anywhere] * 2 + [vm],
             scratch_shapes=[
                 pltpu.VMEM((sketch_rows, depth), F32),
                 pltpu.VMEM((depth, slab), F32),
+                pltpu.VMEM((depth, panel), BF16),
+                pltpu.VMEM((depth, panel), BF16),
+                pltpu.VMEM((R // 2, share, cols_dev + slab), F32),
+                pltpu.VMEM((R // 2, share, cols_dev + slab), F32),
                 pltpu.VMEM((C, MOST, depth), F32),
                 pltpu.VMEM((sketch_rows, cols_dev + slab), F32),
                 pltpu.VMEM((half, half + slab), F32),
@@ -455,7 +490,8 @@
                 pltpu.VMEM((half, half + slab), F32),
                 pltpu.VMEM((half, half), F32),
                 pltpu.VMEM((C, share, panel), F32),
-                dma((2,)),
+                dma((4,)),
+                *[dma((R // 2,))] * 2,
                 *[dma((PARTS,))] * 6,
                 *[dma((R - 1,))] * 10,
                 *[dma((C - 1,))] * 2,
@@ -497,15 +533,16 @@
                 collective_id=0, has_side_effects=True, vmem_limit_bytes=56 * 1024 * 1024),
         )(matrix, gaussian, pivots.reshape(1, panel), trailing)
         place = jnp.eye(panel, dtype=BF16)
-    coupling, projected, tsk = pl.pallas_call(
+    return pl.pallas_call(
         solve_and_project,
         out_shape=[
+            jax.ShapeDtypeStruct((share, cols_dev), F32),
             jax.ShapeDtypeStruct((panel, slab), F32),
             jax.ShapeDtypeStruct((depth, slab), F32),
             jax.ShapeDtypeStruct((share, slab), F32),
         ],
-        in_specs=[vm] * 4 + [anywhere] * 3,
-        out_specs=[vm] * 3,
+        in_specs=[vm] * 5 + [anywhere] * 3,
+        out_specs=[vm] * 4,
         scratch_shapes=[
             pltpu.VMEM((depth, panel), BF16),
             pltpu.VMEM((depth, panel), BF16),
@@ -513,8 +550,7 @@
             dma((3,)),
         ],
         compiler_params=pltpu.CompilerParams(vmem_limit_bytes=56 * 1024 * 1024),
-    )(sums, gtrail, gpan, place, phi, plo, trailing)
-    return sketch, coupling, projected, tsk
+    )(sums, gtrail, gpan, place, sketch, phi, plo, trailing)
 
 
 def solution(mesh):

time: 52.8 us -> 48.6 us (0.920)
  Pallas kernels: 51.3 us -> 47.8 us
  local copies, waits for them, and re-layouts: 0.62 us -> 0 us
    pallas_call x1, Pallas kernels: 39.4 us -> 35.9 us  [shards(): pl.pallas_call(functools.partial(gather_by_halves, R, C), out_shape=[jax....]
    unnamed x3 -> x0, local copies, waits for them, and re-layouts: 0.62 us -> none
where the time goes in v4:
time: 48.6 us; the launch traced here: 48.5 us
  Pallas kernels  47.8 us (98%)
  between operations  0.64 us (1%)
    pallas_call x1, Pallas kernels, shards(): pl.pallas_call(functools.partial(gather_by_halves, R, C), out_shape=[jax....  35.9 us
    pallas_call x1, Pallas kernels, shards(): pl.pallas_call(solve_and_project, out_shape=[jax.ShapeDtypeStruct((share,...  11.9 us

profile of v4, /device:TPU:0, one launch (start us, length us, event | category | flops | bytes accessed | tf_op | source)
XLA Modules:
  0.0 48.5 jit_solution(18418048749292737037)
XLA Ops:
  0.6 35.9 %shard_map.75 = (f32[32,256]{1,0:T(8,128)}, f32[32,128]{1,0:T(8,128)}, f32[32,256]{1,0:T(8,128)}, f32[256,384]{1,0:T(8,128)}, bf16[2048,256]{1,0:T(8,128)(2,1)},...) custom-call(f32[2048,256]{1,0:T(8,128)} %mat.1, f32[256,2048]{1,0:T(8,128)} %gau_in.1, s32[1,256]{1,0:T(1,128)} %bitcast.1, ...), custom_call_target="tpu_custom_call" | custom-call | tf_op jit(solution)/shard_map/pallas_call | solution.py:462
  36.5 11.9 %shard_map.76 = (f32[32,256]{1,0:T(8,128)}, f32[256,128]{1,0:T(8,128)}, f32[2048,128]{1,0:T(8,128)}, f32[32,128]{1,0:T(8,128)}) custom-call(f32[256,384]{1,0:T(8,128)} %get-tuple-element.11.sums, f32[32,128]{1,0:T(8,128)} %get-tuple-element.12.gtrail, f32[32,256]{1,0:T(8,128)} %get-tuple-element.13.gpan, bf16[256,256]{1,0:T(8,128)(2,1)} %get-tuple-element.14.place, ...), custom_call_target="tpu_custom_call" | custom-call | tf_op jit(solution)/shard_map/pallas_call | solution.py:536

commit v5 on v4

--- a/solution.py
+++ b/solution.py
@@ -311,11 +311,28 @@
             device_id=(2 * to + side, c), device_id_type=MESH)
         cp.start()
         sketch_out.append(cp)
-    for q in range(1, PARTS):
-        across[q].wait_recv()
-        relays[q].start()
-    own_t = jnp.transpose(own)
-    t_high, t_low = split(own_t)
+    across[1].wait_recv()
+    relays[1].start()
+
+    group = MOST // 2
+
+    def far_sums(h):
+        for q in range(h * PARTS // 2, (h + 1) * PARTS // 2):
+            relays[q].wait_recv()
+        values = gath[pl.ds(2 * (1 - y), 2), h * group:(h + 1) * group].reshape(half // 2, depth)
+        r2 = split(values)
+        far[h, :, :half] = dot3(r2, o2, NT)
+        far[h, :, half:] = dot3(r2, t2)
+        return scatter(far.at[h], in_far.at[h], hsh // 2, o_send.at[h], o_recv.at[h])
+
+    def far_spread(h):
+        total = finish(far_out[h], far.at[h], in_far.at[h], hsh // 2)
+        return spread(total, full_far.at[h], hsh // 2, ao_send.at[h], ao_recv.at[h])
+
+    far_out = [far_sums(0)]
+    across[2].wait_recv()
+    relays[2].start()
+    t_high, t_low = split(jnp.transpose(own))
     hbuf[:, :half] = t_high
     lbuf[:, :half] = t_low
     for cp in near_all:
@@ -323,16 +340,14 @@
     swap = pltpu.make_async_remote_copy(
         full_near.at[:, pl.ds(0, half)], diag, d_send.at[0], d_recv.at[0],
         device_id=(r, opposite), device_id_type=MESH)
+    for q in range(3, PARTS):
+        across[q].wait_recv()
+        relays[q].start()
     swap.start()
-    for cp in relays:
-        cp.wait_recv()
+    far_all = far_spread(0)
+    far_out.append(far_sums(1))
 
     other = gath[pl.ds(2 * (1 - y), 2)].reshape(half, depth)
-    r2 = split(other)
-    far[:, :half] = dot3(r2, o2, NT)
-    far[:, half:] = dot3(r2, t2)
-    far_out = scatter(far, in_far, hsh, o_send, o_recv)
-
     r_high, r_low = split(jnp.transpose(other))
     hbuf[:, half:] = r_high
     lbuf[:, half:] = r_low
@@ -344,7 +359,7 @@
     place = (slot_col == slot).astype(F32).astype(BF16)
     place_o[...] = place
 
-    far_all = spread(finish(far_out, far, in_far, hsh), full_far, hsh, ao_send, ao_recv)
+    far_all = far_all + far_spread(1)
 
     for cp in sketch_out:
         cp.wait_recv()
@@ -365,9 +380,11 @@
     swap.wait_recv()
     for cp in far_all:
         cp.wait_recv()
-    mixed = full_far[:, :half]
+    whole = jnp.concatenate(
+        [full_far[h, i * group:(i + 1) * group] for i in range(2) for h in range(2)], axis=0)
+    mixed = whole[:, :half]
     first_rows = jnp.concatenate([full_near[:, :half], jnp.transpose(mixed), full_near[:, half:]], axis=1)
-    last_rows = jnp.concatenate([mixed, diag[...], full_far[:, half:]], axis=1)
+    last_rows = jnp.concatenate([mixed, diag[...], whole[:, half:]], axis=1)
     by_rows = ordered(place, jnp.concatenate([first_rows, last_rows], axis=0))
     sums_o[:, panel:] = by_rows[:, panel:]
     sums_o[:, :panel] = ordered(place, jnp.transpose(by_rows[:, :panel]))
@@ -377,7 +394,7 @@
     for d in range(1, C):
         gp += gpbuf[d]
     gpan_o[...] = gp
-    for cp in across + beside + relays + near_out + pair_out + sketch_out + near_all + far_out + far_all + third + [swap]:
+    for cp in across + beside + relays + near_out + pair_out + sketch_out + near_all + far_out[0] + far_out[1] + far_all + third + [swap]:
         cp.wait_send()
     for cp in stores:
         cp.wait()
@@ -457,7 +474,7 @@
     vm = pl.BlockSpec(memory_space=pltpu.VMEM)
     anywhere = pl.BlockSpec(memory_space=pl.ANY)
     dma = pltpu.SemaphoreType.DMA
-    if C == 4 and R % 2 == 0 and C * MOST == panel and panel == 2 * slab and (panel // 2) % (8 * R) == 0:
+    if C == 4 and R % 2 == 0 and C * MOST == panel and panel == 2 * slab and panel % (32 * R) == 0:
         half = panel // 2
         sketch, gtrail, gpan, sums, phi, plo, place = pl.pallas_call(
             functools.partial(gather_by_halves, R, C),
@@ -482,18 +499,21 @@
                 pltpu.VMEM((C, MOST, depth), F32),
                 pltpu.VMEM((sketch_rows, cols_dev + slab), F32),
                 pltpu.VMEM((half, half + slab), F32),
-                pltpu.VMEM((half, half + slab), F32),
+                pltpu.VMEM((2, half // 2, half + slab), F32),
                 pltpu.VMEM((R - 1, share, cols_dev + slab), F32),
                 pltpu.VMEM((R - 1, half // R, half + slab), F32),
-                pltpu.VMEM((R - 1, half // R, half + slab), F32),
+                pltpu.VMEM((2, R - 1, half // (2 * R), half + slab), F32),
                 pltpu.VMEM((half, half + slab), F32),
-                pltpu.VMEM((half, half + slab), F32),
+                pltpu.VMEM((2, half // 2, half + slab), F32),
                 pltpu.VMEM((half, half), F32),
                 pltpu.VMEM((C, share, panel), F32),
                 dma((4,)),
                 *[dma((R // 2,))] * 2,
                 *[dma((PARTS,))] * 6,
-                *[dma((R - 1,))] * 10,
+                *[dma((R - 1,))] * 4,
+                *[dma((2, R - 1))] * 2,
+                *[dma((R - 1,))] * 2,
+                *[dma((2, R - 1))] * 2,
                 *[dma((C - 1,))] * 2,
                 *[dma((1,))] * 2,
             ],

time: 48.6 us -> 52.4 us (1.078)
  Pallas kernels: 47.8 us -> 51.4 us
    pallas_call x1, Pallas kernels: 35.9 us -> 39.3 us  [shards(): pl.pallas_call(functools.partial(gather_by_halves, R, C), out_shape=[jax....]
where the time goes in v5:
time: 52.4 us; the launch traced here: 52.2 us
  Pallas kernels  51.4 us (98%)
  between operations  0.8 us (2%)
    pallas_call x1, Pallas kernels, shards(): pl.pallas_call(functools.partial(gather_by_halves, R, C), out_shape=[jax....  39.3 us
    pallas_call x1, Pallas kernels, shards(): pl.pallas_call(solve_and_project, out_shape=[jax.ShapeDtypeStruct((share,...  12.1 us

profile of v5, /device:TPU:0, one launch (start us, length us, event | category | flops | bytes accessed | tf_op | source)
XLA Modules:
  0.0 52.2 jit_solution(5830094234062537078)
XLA Ops:
  0.6 39.3 %shard_map.75 = (f32[32,256]{1,0:T(8,128)}, f32[32,128]{1,0:T(8,128)}, f32[32,256]{1,0:T(8,128)}, f32[256,384]{1,0:T(8,128)}, bf16[2048,256]{1,0:T(8,128)(2,1)},...) custom-call(f32[2048,256]{1,0:T(8,128)} %mat.1, f32[256,2048]{1,0:T(8,128)} %gau_in.1, s32[1,256]{1,0:T(1,128)} %bitcast.1, ...), custom_call_target="tpu_custom_call" | custom-call | tf_op jit(solution)/shard_map/pallas_call | solution.py:479
  40.0 12.1 %shard_map.76 = (f32[32,256]{1,0:T(8,128)}, f32[256,128]{1,0:T(8,128)}, f32[2048,128]{1,0:T(8,128)}, f32[32,128]{1,0:T(8,128)}) custom-call(f32[256,384]{1,0:T(8,128)} %get-tuple-element.11.sums, f32[32,128]{1,0:T(8,128)} %get-tuple-element.12.gtrail, f32[32,256]{1,0:T(8,128)} %get-tuple-element.13.gpan, bf16[256,256]{1,0:T(8,128)(2,1)} %get-tuple-element.14.place, ...), custom_call_target="tpu_custom_call" | custom-call | tf_op jit(solution)/shard_map/pallas_call | solution.py:556

commit v6 on v4

--- a/solution.py
+++ b/solution.py
@@ -312,12 +312,13 @@
         cp.start()
         sketch_out.append(cp)
     for q in range(1, PARTS):
+        if q == PARTS - 1:
+            own_t = jnp.transpose(own)
+            t_high, t_low = split(own_t)
+            hbuf[:, :half] = t_high
+            lbuf[:, :half] = t_low
         across[q].wait_recv()
         relays[q].start()
-    own_t = jnp.transpose(own)
-    t_high, t_low = split(own_t)
-    hbuf[:, :half] = t_high
-    lbuf[:, :half] = t_low
     for cp in near_all:
         cp.wait_recv()
     swap = pltpu.make_async_remote_copy(

time: 48.6 us -> 48.6 us (level)
  no operation moved by 1% of the time
where the time goes in v6:
time: 48.6 us; the launch traced here: 48.5 us
  Pallas kernels  47.8 us (98%)
  between operations  0.64 us (1%)
    pallas_call x1, Pallas kernels, shards(): pl.pallas_call(functools.partial(gather_by_halves, R, C), out_shape=[jax....  35.9 us
    pallas_call x1, Pallas kernels, shards(): pl.pallas_call(solve_and_project, out_shape=[jax.ShapeDtypeStruct((share,...  11.9 us

profile of v6, /device:TPU:0, one launch (start us, length us, event | category | flops | bytes accessed | tf_op | source)
XLA Modules:
  0.0 48.5 jit_solution(8499955680626074665)
XLA Ops:
  0.6 35.9 %shard_map.75 = (f32[32,256]{1,0:T(8,128)}, f32[32,128]{1,0:T(8,128)}, f32[32,256]{1,0:T(8,128)}, f32[256,384]{1,0:T(8,128)}, bf16[2048,256]{1,0:T(8,128)(2,1)},...) custom-call(f32[2048,256]{1,0:T(8,128)} %mat.1, f32[256,2048]{1,0:T(8,128)} %gau_in.1, s32[1,256]{1,0:T(1,128)} %bitcast.1, ...), custom_call_target="tpu_custom_call" | custom-call | tf_op jit(solution)/shard_map/pallas_call | solution.py:463
  36.5 11.9 %shard_map.76 = (f32[32,256]{1,0:T(8,128)}, f32[256,128]{1,0:T(8,128)}, f32[2048,128]{1,0:T(8,128)}, f32[32,128]{1,0:T(8,128)}) custom-call(f32[256,384]{1,0:T(8,128)} %get-tuple-element.11.sums, f32[32,128]{1,0:T(8,128)} %get-tuple-element.12.gtrail, f32[32,256]{1,0:T(8,128)} %get-tuple-element.13.gpan, bf16[256,256]{1,0:T(8,128)(2,1)} %get-tuple-element.14.place, ...), custom_call_target="tpu_custom_call" | custom-call | tf_op jit(solution)/shard_map/pallas_call | solution.py:537
